TPU v7x, 32 devices: a whole 2x2x4 slice. The times are simulated.
32 devices in a mesh: row: 4 (over y, core), col: 8 (over z, x).
Axes of the slice: x: 2, y: 2, z: 4, core: 2. Of those that a mesh axis runs over, the one named last changes fastest.
Arguments:
- mock_maps: bfloat16 [512, 40960], P('col', 'row'), may hold values from -6 to 6
- window_blocks: int32 [4], replicated, may hold values from 0 to 31, as said below
- kept_tiles: int32 [32, 4], P(('row', 'col')), may hold values from 0 to 1, as said below
- taper_index: int32 [32, 4], P(('row', 'col')), may hold values from 0 to 3, as said below
- taper_table: float32 [4], replicated, may hold values from 0.25 to 2
Outputs:
- covariance: bfloat16 [40960, 5120], P(('row', 'col'))
Inputs may be any that keep to these rules, and one draw needn't show every extreme that they name: `window_blocks`: the entries are distinct feature blocks; the first and the last feature block are always among them. `kept_tiles`: A tile whose row block is its own window column block is always kept. `taper_index`: A tile whose row block is its own window column block takes entry 0.
All inputs are finite; a program needn't handle non-finite values.
Results may differ from a plain program's by a relative error of at most 0.001.
Values may be sent and summed in bfloat16 or wider, within the bound.
A program may use at most 128 MiB of HBM per device.

v0:
```python
import jax
import jax.numpy as jnp
from jax import lax
from jax.sharding import PartitionSpec as P

WINDOW = 4


def per_device(mock_maps, window_blocks, kept_tiles, taper_index, taper_table):
    own_block = lax.all_to_all(mock_maps, "col", split_axis=1, concat_axis=0, tiled=True)
    mock_count = own_block.shape[0]
    block_width = own_block.shape[1]
    own_mean = jnp.sum(own_block, axis=0, dtype=jnp.float32) / mock_count
    col_count = lax.axis_size("col")
    row_here = lax.axis_index("row")
    slices = []
    for slot in range(WINDOW):
        block_id = window_blocks[slot]
        local_start = block_id % col_count * block_width
        piece = lax.dynamic_slice_in_dim(mock_maps, local_start, block_width, 1).astype(jnp.float32)
        slices.append(jnp.where(block_id // col_count == row_here, piece, jnp.float32(0.0)))
    stacked = lax.psum(jnp.concatenate(slices, axis=1).astype(jnp.bfloat16), "row")
    piece = lax.all_gather(stacked, "col", axis=0, tiled=True)
    total = lax.dot_general(
        own_block, piece, (((0,), (0,)), ((), ())), preferred_element_type=jnp.float32
    )
    column_sum = jnp.sum(piece, axis=0, dtype=jnp.float32)
    products, column_sum = (total, column_sum)
    panel_mean = column_sum / mock_count
    classes = jnp.arange(taper_table.shape[0], dtype=jnp.int32)
    weights = jnp.sum(
        jnp.where(
            classes[None, :] == taper_index[0][:, None], taper_table[None, :], jnp.float32(0.0)
        ),
        axis=1,
    )
    weight_cols = jnp.repeat(weights, block_width)
    keep_cols = jnp.repeat(kept_tiles[0], block_width)
    centred = products - mock_count * own_mean[:, None] * panel_mean[None, :]
    tile_value = weight_cols[None, :] * centred / (mock_count - 1)
    tile_value = jnp.where(keep_cols[None, :] > 0, tile_value, jnp.float32(0.0))
    return tile_value.astype(jnp.bfloat16)


def solution(mesh):
    in_specs = (P("col", "row"), P(), P(("row", "col"), None), P(("row", "col"), None), P())
    out_specs = P(("row", "col"), None)
    return jax.shard_map(
        per_device, mesh=mesh, in_specs=in_specs, out_specs=out_specs, check_vma=False
    )
```

profile of v0, /device:TPU:1, one launch (start us, length us, event | category | flops | bytes accessed | tf_op | source)
XLA Modules:
  0.0 205.0 jit_solution(15451969285660215913)
XLA Ops:
  6.5 0.0 copy-start.1
  6.5 0.0 all-reduce.2.cloned.1.call-start
  6.5 1.4 fusion.4
  18.1 1.3 select_convert_fusion.3
  19.4 0.9 pad_maximum_fusion
  20.3 0.0 all-reduce.2.cloned.1.call-update
  20.3 0.0 all-gather.2.cloned.1.call-start
  20.4 34.7 %all-reduce.2.cloned.1.call-done = bf16[64,5120]{1,0:T(8,128)(2,1)} async-done(((bf16[64,5120]{1,0:T(8,128)(2,1)}), bf16[64,5120]{1,0:T(8,128)(2,1)}) %all-reduce.2.cloned.1.call-update) | async-done | bytes 655376 | tf_op jit(solution)/shard_map/psum | solution.py:22
  55.1 0.0 all-gather.2.cloned.1.call-update
  55.1 2.5 %copy.16 = bf16[8,8,8,1280]{3,2,0,1:T(8,128)(2,1)} copy(bf16[8,8,8,1280]{3,2,1,0:T(8,128)(2,1)} %bitcast.28) | data formatting | bytes 2621440 | tf_op jit(solution)/shard_map/all_to_all | solution.py:10
  57.5 5.6 %all-to-all-start = ((bf16[64,8,1280]{2,0,1:T(8,128)(2,1)}), bf16[64,8,1280]{2,0,1:T(8,128)(2,1)S(1)}, u32[]{:S(2)}, u32[]{:S(2)}) async-start(bf16[64,8,1280]{2,0,1:T(8,128)(2,1)} %bitcast.26), calls=%async_computation | async-start | bytes 2621440 | tf_op jit(solution)/shard_map/all_to_all | solution.py:10
  63.1 0.0 copy-done.1
  63.2 0.1 broadcast_in_dim.41
  63.3 0.0 copy-done.2
  63.3 0.0 copy-done.3
  63.3 0.2 select_reduce_fusion
  63.4 0.1 broadcast_in_dim.45
  63.5 49.0 %all-to-all-done = bf16[64,8,1280]{2,0,1:T(8,128)(2,1)S(1)} async-done(((bf16[64,8,1280]{2,0,1:T(8,128)(2,1)}), bf16[64,8,1280]{2,0,1:T(8,128)(2,1)S(1)}, u32[]{:S(2)}, u32[]{:S(2)}) %all-to-all-start) | async-done | bytes 1310752 | tf_op jit(solution)/shard_map/all_to_all | solution.py:10
  112.5 0.2 convert_reduce_fusion.1
  112.8 52.5 %all-gather.2.cloned.1.call-done = bf16[512,5120]{1,0:T(8,128)(2,1)} async-done(((bf16[64,5120]{1,0:T(8,128)(2,1)}), bf16[512,5120]{1,0:T(8,128)(2,1)}) %all-gather.2.cloned.1.call-update) | async-done | bytes 5242896 | tf_op jit(solution)/shard_map/all_gather | solution.py:23
  165.2 3.9 %convert_reduce_fusion = f32[5120]{0:T(1024)S(1)} fusion(bf16[512,5120]{1,0:T(8,128)(2,1)} %all-gather.2.cloned.1.call-done), kind=kLoop, calls=%fused_computation.5 | loop fusion | flops 5237760 | bytes 5263360 | tf_op jit(solution)/shard_map/reduce_sum | solution.py:27
  169.1 0.1 copy-done
  169.3 11.2 %fusion.3 = bf16[1280,5120]{0,1:T(8,128)(2,1)} fusion(bf16[512,5120]{1,0:T(8,128)(2,1)S(1)} %copy-done, bf16[512,1280]{1,0:T(8,128)(2,1)S(1)} %bitcast.27, f32[5120]{0:T(1024)S(1)} %broadcast_multiply_fusion, f32[1280]{0:T(1024)S(1)} %convert_reduce_fusion.1, f32[5120]{0:T(1024)S(1)} %mul.39, pred[5120]{0:T(1024)(128)(4,1)S(1)} %gt.21), kind=kOutput, calls=%fused_computation.4 | convolution fusion | flops 6750208000 | bytes 19712000 | tf_op jit(solution)/shard_map/dot_general | solution.py:24
  180.5 17.6 %copy.13 = bf16[1280,5120]{1,0:T(8,128)(2,1)} copy(bf16[1280,5120]{0,1:T(8,128)(2,1)} %fusion.3) | data formatting | bytes 26214400 | tf_op jit(solution)/shard_map/convert_element_type | solution.py:42
  (7 shorter events, 0.0 us)
Async XLA Ops:
  6.5 56.6 %copy-start.1 = (s32[1,4]{1,0:T(1,128)S(1)}, s32[1,4]{1,0:T(1,128)}, u32[]{:S(2)}) copy-start(s32[1,4]{1,0:T(1,128)} %param.7) | copy-start | bytes 52
  6.5 56.7 %copy-start.2 = (f32[4]{0:T(128)S(1)}, f32[4]{0:T(128)}, u32[]{:S(2)}) copy-start(f32[4]{0:T(128)} %param.9) | copy-start | bytes 52
  6.5 56.7 %copy-start.3 = (s32[1,4]{1,0:T(1,128)S(1)}, s32[1,4]{1,0:T(1,128)}, u32[]{:S(2)}) copy-start(s32[1,4]{1,0:T(1,128)} %param.8) | copy-start | bytes 52
  6.5 48.5 %all-reduce.2.cloned.1.call-start = ((), (), s32[]{:S(2)}) async-start(), calls=%async_computation.1 | async-start | bytes 1310720 | tf_op jit(solution)/shard_map/psum | solution.py:22
  20.3 144.9 %all-gather.2.cloned.1.call-start = ((), (), s32[]{:S(2)}) async-start(), calls=%async_computation.2 | async-start | bytes 5898240 | tf_op jit(solution)/shard_map/all_gather | solution.py:23
  57.5 55.0 %all-to-all-start = ((bf16[64,8,1280]{2,0,1:T(8,128)(2,1)}), bf16[64,8,1280]{2,0,1:T(8,128)(2,1)S(1)}, u32[]{:S(2)}, u32[]{:S(2)}) async-start(bf16[64,8,1280]{2,0,1:T(8,128)(2,1)} %bitcast.26), calls=%async_computation | async-start | bytes 2621440 | tf_op jit(solution)/shard_map/all_to_all | solution.py:10
  165.2 4.0 %copy-start = (bf16[512,5120]{1,0:T(8,128)(2,1)S(1)}, bf16[512,5120]{1,0:T(8,128)(2,1)}, u32[]{:S(2)}) copy-start(bf16[512,5120]{1,0:T(8,128)(2,1)} %all-gather.2.cloned.1.call-done) | copy-start | bytes 15728644
Sparse Core Ops, SparseCore 0:
  20.4 34.5 all-reduce.1
  57.2 107.9 all-gather.1
where the time goes:
time: 207 us; the launch traced here: 205 us
  waiting for transfers between devices  136 us (66%)
  between operations  23.6 us (11%)
  local copies, waits for them, and re-layouts  21.9 us (11%)
  matrix products  11.2 us (5%)
  other arithmetic  6.44 us (3%)
  starting transfers between devices  5.64 us (3%)
    all_gather x1, waiting for transfers between devices, per_device(): piece = lax.all_gather(stacked, 'col', axis=0, tiled=True)  52.5 us
    all_to_all x1, waiting for transfers between devices, per_device(): lax.all_to_all(mock_maps, 'col', split_axis=1, concat_axis=0, tiled=True)  49 us
    psum x1, waiting for transfers between devices, per_device(): lax.psum(jnp.concatenate(slices, axis=1).astype(jnp.bfloat16), 'row')  34.7 us
    convert_element_type x1, local copies, waits for them, and re-layouts, per_device(): return tile_value.astype(jnp.bfloat16)  17.6 us
    dot_general x1, matrix products, per_device(): lax.dot_general(own_block, piece, (((0,), (0,)), ((), ())), preferred_ele...  11.2 us
    all_to_all x1, starting transfers between devices, per_device(): lax.all_to_all(mock_maps, 'col', split_axis=1, concat_axis=0, tiled=True)  5.6 us
  transfers between devices with their start and end apart: 3, of which 3 were waited for; matrix products, arithmetic and copies ran while one was open for 1% of the time, Pallas kernels for 0%

commit v1 on v0

v1 whole, which is shorter than its diff:
```python
import functools

import jax
import jax.numpy as jnp
from jax import lax
from jax.experimental import pallas as pl
from jax.experimental.pallas import tpu as pltpu
from jax.sharding import PartitionSpec as P

MESH = pl.DeviceIdType.MESH
WINDOW = 4
CORES = 2
ALONG_Z = 4


def window_kernel(row_count, col_count, window_ref, maps_ref, held_ref):
    row = lax.axis_index("row")
    width = maps_ref.shape[1] // col_count
    part = held_ref.shape[3]
    for r in range(row_count):
        first = r * part
        block = window_ref[first // width]
        start = pl.multiple_of(lax.rem(block, col_count) * width + first % width, 128)
        here = lax.div(block, col_count) == row

        @pl.when(here)
        def _():
            held_ref[r % CORES, r // CORES] = maps_ref[:, pl.ds(start, part)]

        @pl.when(jnp.logical_not(here))
        def _():
            held_ref[r % CORES, r // CORES] = jnp.zeros(held_ref.shape[2:], held_ref.dtype)


def gather_kernel(
    row_count, col_count, held_ref, maps_ref, own_ref, panels_ref,
    from_twin, summed, from_y, piece,
    twin_send, twin_recv, ysum_send, ysum_recv,
    z_send, x_send, y_send, core_send, panel_recv,
    own_send, own_recv, local_sem,
):
    ny, nx, nz = row_count // CORES, col_count // ALONG_Z, ALONG_Z
    row, col = lax.axis_index("row"), lax.axis_index("col")
    y, core = row // CORES, row % CORES
    z, x = col // nx, col % nx
    twin = y * CORES + (1 - core)
    width = own_ref.shape[2]
    part = panels_ref.shape[3]

    def row_of(d):
        return lax.rem(y + d, ny) * CORES + core

    barrier = pltpu.get_barrier_semaphore()
    peers = [(row, lax.rem(col + d, col_count)) for d in range(1, col_count)]
    peers += [(twin, col)] + [(row_of(d), col) for d in range(1, ny)]
    for peer in peers:
        pl.semaphore_signal(barrier, inc=1, device_id=peer, device_id_type=MESH)

    pl.semaphore_wait(barrier, len(peers))

    started = []

    def send(src, dst, send_sem, recv_sem, device):
        copy = pltpu.make_async_remote_copy(
            src_ref=src, dst_ref=dst, send_sem=send_sem, recv_sem=recv_sem,
            device_id=device, device_id_type=MESH,
        )
        copy.start()
        return copy

    def send_own(d):
        dest = lax.rem(col + d, col_count)
        columns = pl.ds(pl.multiple_of(dest * width, 128), width)
        started.append(send(
            maps_ref.at[:, columns], own_ref.at[col],
            own_send.at[d], own_recv.at[col], (row, dest),
        ))

    pending = list(range(1, col_count))
    pending.sort(key=lambda d: -abs(d - col_count // 2))
    pending = pending[::-1]

    def send_some(count):
        for _ in range(min(count, len(pending))):
            send_own(pending.pop(0))

    twin_copy = send(held_ref.at[1 - core], from_twin, twin_send, twin_recv, (twin, col))
    keep_own = pltpu.make_async_copy(
        maps_ref.at[:, pl.ds(pl.multiple_of(col * width, 128), width)], own_ref.at[col], local_sem.at[0]
    )
    keep_own.start()
    twin_copy.wait_recv()
    for d in range(ny):
        part_y = lax.rem(y + d, ny)
        summed[d] = held_ref[core, part_y] + from_twin[part_y]
    for d in range(1, ny):
        started.append(send(
            summed.at[d], from_y.at[ny - d], ysum_send.at[d], ysum_recv.at[ny - d], (row_of(d), col)
        ))
    send_some(2)
    total = summed[0]
    for d in range(1, ny):
        pltpu.make_async_remote_copy(
            src_ref=summed.at[d], dst_ref=from_y.at[d], send_sem=ysum_send.at[d],
            recv_sem=ysum_recv.at[d], device_id=(row, col), device_id_type=MESH,
        ).wait_recv()
        total = total + from_y[d]
    piece[...] = total
    keep_piece = pltpu.make_async_copy(piece, panels_ref.at[row, col], local_sem.at[1])
    keep_piece.start()

    def slot(r, c):
        return panels_ref.at[r, c]

    def arrived(r, c):
        pltpu.make_async_remote_copy(
            src_ref=slot(r, c), dst_ref=slot(r, c), send_sem=core_send.at[r, c],
            recv_sem=panel_recv.at[r, c], device_id=(row, col), device_id_type=MESH,
        ).wait_recv()

    def out(src, r, c, send_sem, device, waiting):
        copy = pltpu.make_async_remote_copy(
            src_ref=src, dst_ref=slot(r, c), send_sem=send_sem,
            recv_sem=panel_recv.at[r, c], device_id=device, device_id_type=MESH,
        )
        if waiting:
            copy.wait_send()
        else:
            copy.start()

    def z_out(src, zz, up, waiting):
        to = z + 1 if up else z - 1

        @pl.when(to < nz if up else to >= 0)
        def _():
            c = zz * nx + x
            out(src, row, c, z_send.at[int(up), zz], (row, to * nx + x), waiting)

    def x_out(src, zz, waiting):
        c = zz * nx + x
        for d in range(1, nx):
            out(src, row, c, x_send.at[d, zz], (row, z * nx + lax.rem(x + d, nx)), waiting)

    def y_out(src, c, waiting):
        for d in range(1, ny):
            out(src, row, c, y_send.at[d, c], (row_of(d), col), waiting)

    def core_out(src, r, c, waiting):
        out(src, r, c, core_send.at[r, c], (twin, col), waiting)

    def at_z(d, body):
        if d == 0:
            body(z, None)
            return

        @pl.when(z >= d)
        def _():
            body(z - d, True)

        @pl.when(z + d < nz)
        def _():
            body(z + d, False)

    def z_event(waiting, zz, up):
        c = zz * nx + x
        if up is None:
            src = piece
            z_out(src, zz, True, waiting)
            z_out(src, zz, False, waiting)
        else:
            src = slot(row, c)
            if not waiting:
                arrived(row, c)
            z_out(src, zz, up, waiting)
        y_out(src, c, waiting)
        x_out(src, zz, waiting)
        core_out(src, row, c, waiting)

    def x_event(waiting, zz, up):
        for d in range(1, nx):
            c = zz * nx + lax.rem(x + d, nx)
            if not waiting:
                arrived(row, c)
            y_out(slot(row, c), c, waiting)
            core_out(slot(row, c), row, c, waiting)

    def y_event(waiting, own_x, zz, up):
        for dx in ([0] if own_x else range(1, nx)):
            c = zz * nx + lax.rem(x + dx, nx)
            for d in range(1, ny):
                r = row_of(d)
                if not waiting:
                    arrived(r, c)
                core_out(slot(r, c), r, c, waiting)

    def events(waiting):
        at_z(0, functools.partial(z_event, waiting))
        if not waiting:
            send_some(2)
        for d in range(1, nz):
            at_z(d, functools.partial(z_event, waiting))
            at_z(d - 1, functools.partial(x_event, waiting))
            if not waiting:
                send_some(1 if d < nz - 1 else col_count)
        at_z(nz - 1, functools.partial(x_event, waiting))
        for d in range(nz):
            at_z(d, functools.partial(y_event, waiting, True))
            at_z(d, functools.partial(y_event, waiting, False))

    events(False)

    for d in range(ny):
        r = lax.rem(y + d, ny) * CORES + (1 - core)

        @pl.loop(0, col_count)
        def _(c):
            arrived(r, c)

    for d in range(1, col_count):
        source = lax.rem(col + d, col_count)
        pltpu.make_async_remote_copy(
            src_ref=own_ref.at[source], dst_ref=own_ref.at[source], send_sem=own_send.at[d],
            recv_sem=own_recv.at[source], device_id=(row, source), device_id_type=MESH,
        ).wait_recv()
    twin_copy.wait_send()
    for copy in started:
        copy.wait_send()
    events(True)
    keep_own.wait()
    keep_piece.wait()


def gather(mock_maps, window_blocks, row_count, col_count):
    mocks = mock_maps.shape[0]
    width = mock_maps.shape[1] // col_count
    part = WINDOW * width // row_count
    ny = row_count // CORES
    nx = col_count // ALONG_Z
    dma = pltpu.SemaphoreType.DMA
    vmem = pl.BlockSpec(memory_space=pltpu.VMEM)
    held = pl.pallas_call(
        functools.partial(window_kernel, row_count, col_count),
        out_shape=jax.ShapeDtypeStruct((CORES, ny, mocks, part), jnp.bfloat16),
        in_specs=[pl.BlockSpec(memory_space=pltpu.SMEM), vmem],
        out_specs=vmem,
        name="window",
    )(window_blocks, mock_maps)
    return pl.pallas_call(
        functools.partial(gather_kernel, row_count, col_count),
        out_shape=(
            jax.ShapeDtypeStruct((col_count, mocks, width), jnp.bfloat16),
            jax.ShapeDtypeStruct((row_count, col_count, mocks, part), jnp.bfloat16),
        ),
        in_specs=[vmem, vmem],
        out_specs=(pl.BlockSpec(memory_space=pl.ANY), pl.BlockSpec(memory_space=pl.ANY)),
        scratch_shapes=[
            pltpu.VMEM((ny, mocks, part), jnp.bfloat16),
            pltpu.VMEM((ny, mocks, part), jnp.bfloat16),
            pltpu.VMEM((ny, mocks, part), jnp.bfloat16),
            pltpu.VMEM((mocks, part), jnp.bfloat16),
            dma, dma, dma((ny,)), dma((ny,)),
            dma((2, ALONG_Z)), dma((nx, ALONG_Z)), dma((ny, col_count)),
            dma((row_count, col_count)), dma((row_count, col_count)),
            dma((col_count,)), dma((col_count,)), dma((2,)),
        ],
        compiler_params=pltpu.CompilerParams(
            collective_id=0, has_side_effects=True, vmem_limit_bytes=32 * 2**20
        ),
        name="gather",
    )(held, mock_maps)


def tile_kernel(chunks_per_block, kept_ref, index_ref, table_ref, own_ref, panel_ref, out_ref, own_t, own_sum):
    step = pl.program_id(0)
    slot = step // chunks_per_block
    count, width = own_ref.shape

    @pl.when(step == 0)
    def _():
        own_t[...] = own_ref[...].T
        own_sum[...] = jnp.dot(
            own_t[...], jnp.ones((count, 128), jnp.bfloat16), preferred_element_type=jnp.float32
        )

    kept = kept_ref[0, slot] > 0

    @pl.when(kept)
    def _():
        panel = panel_ref[0]
        scale = table_ref[index_ref[0, slot]] / (count - 1)
        panel_mean = jnp.sum(panel.astype(jnp.float32), axis=0, keepdims=True) / count
        rows = 256
        for first in range(0, width, rows):
            here = slice(first, min(first + rows, width))
            products = jnp.dot(own_t[here, :], panel, preferred_element_type=jnp.float32)
            centred = products - own_sum[here, :1] * panel_mean
            out_ref[here, :] = (scale * centred).astype(jnp.bfloat16)

    @pl.when(jnp.logical_not(kept))
    def _():
        out_ref[...] = jnp.zeros_like(out_ref)


def tiles(own, panels, kept_tiles, taper_index, taper_table):
    count, width = own.shape
    parts, _, part = panels.shape
    chunk = part if part <= 640 else 640
    per_part = part // chunk
    smem = pl.BlockSpec(memory_space=pltpu.SMEM)
    steps = parts * per_part
    return pl.pallas_call(
        functools.partial(tile_kernel, width // chunk),
        grid=(steps,),
        out_shape=jax.ShapeDtypeStruct((width, parts * part), jnp.bfloat16),
        in_specs=[
            smem, smem, smem,
            pl.BlockSpec((count, width), lambda i: (0, 0)),
            pl.BlockSpec((1, count, chunk), lambda i: (i // per_part, 0, i % per_part)),
        ],
        out_specs=pl.BlockSpec((width, chunk), lambda i: (0, i)),
        scratch_shapes=[
            pltpu.VMEM((width, count), jnp.bfloat16),
            pltpu.VMEM((width, 128), jnp.float32),
        ],
        compiler_params=pltpu.CompilerParams(
            dimension_semantics=("arbitrary",), vmem_limit_bytes=40 * 2**20
        ),
        name="tiles",
    )(kept_tiles, taper_index, taper_table, own, panels)


def per_device(row_count, col_count, mock_maps, window_blocks, kept_tiles, taper_index, taper_table):
    own, panels = gather(mock_maps, window_blocks, row_count, col_count)
    own = own.reshape(-1, own.shape[-1])
    panels = panels.reshape(panels.shape[0], -1, panels.shape[-1])
    return tiles(own, panels, kept_tiles, taper_index, taper_table)


def solution(mesh):
    in_specs = (P("col", "row"), P(), P(("row", "col"), None), P(("row", "col"), None), P())
    out_specs = P(("row", "col"), None)
    return jax.shard_map(
        functools.partial(per_device, mesh.shape["row"], mesh.shape["col"]),
        mesh=mesh, in_specs=in_specs, out_specs=out_specs, check_vma=False,
    )
```

time: 207 us -> 78 us (0.38)
  the two profiles are of different devices: /device:TPU:1 before, /device:TPU:0 now
where the time goes in v1:
time: 78 us; the launch traced here: 77.4 us
  Pallas kernels  73 us (94%)
  local copies, waits for them, and re-layouts  4.36 us (6%)
    pallas_call x1, Pallas kernels, gather(): pl.pallas_call(functools.partial(gather_kernel, row_count, col_count), ou...  60.4 us
    pallas_call x1, Pallas kernels, tiles(): pl.pallas_call(functools.partial(tile_kernel, width // chunk), grid=(step...  10.3 us
    unnamed x10, local copies, waits for them, and re-layouts  4.36 us
    pallas_call x1, Pallas kernels, gather(): pl.pallas_call(functools.partial(window_kernel, row_count, col_count), ou...  2.26 us

profile of v1, /device:TPU:0, one launch (start us, length us, event | category | flops | bytes accessed | tf_op | source)
XLA Modules:
  0.0 77.4 jit_solution(9157380456609024725)
XLA Ops:
  0.0 2.3 %window.1.held_ref = bf16[2,2,64,1280]{3,2,1,0:T(8,128)(2,1)} custom-call(s32[4]{0:T(128)} %window_ref.1, bf16[64,10240]{1,0:T(8,128)(2,1)} %maps_ref.3), custom_call_target="tpu_custom_call" | custom-call | tf_op jit(solution)/shard_map/window/pallas_call | solution.py:241
  2.3 0.0 copy-start
  2.3 1.3 %copy-done = bf16[64,10240]{1,0:T(8,128)(2,1)S(1)} copy-done((bf16[64,10240]{1,0:T(8,128)(2,1)S(1)}, bf16[64,10240]{1,0:T(8,128)(2,1)}, u32[]{:S(2)}) %copy-start) | copy-done | bytes 1310744
  3.6 0.0 copy-start.1
  3.6 1.1 %copy-done.1 = bf16[2,2,64,1280]{3,2,1,0:T(8,128)(2,1)S(1)} copy-done((bf16[2,2,64,1280]{3,2,1,0:T(8,128)(2,1)S(1)}, bf16[2,2,64,1280]{3,2,1,0:T(8,128)(2,1)}, u32[]{:S(2)}) %copy-start.1) | copy-done | bytes 655384
  4.7 60.4 %gather.1 = (bf16[8,64,1280]{2,1,0:T(8,128)(2,1)S(1)}, bf16[4,8,64,1280]{3,2,1,0:T(8,128)(2,1)S(1)}) custom-call(bf16[2,2,64,1280]{3,2,1,0:T(8,128)(2,1)S(1)} %copy-done.1, bf16[64,10240]{1,0:T(8,128)(2,1)S(1)} %copy-done), custom_call_target="tpu_custom_call" | custom-call | tf_op jit(solution)/shard_map/gather/pallas_call | solution.py:248
  65.1 0.0 copy-start.2
  65.1 0.6 copy-done.2
  65.7 0.0 copy-start.3
  65.7 0.7 copy-done.3
  66.4 0.0 copy-start.4
  66.4 0.7 copy-done.4
  67.0 10.3 %tiles.1 = bf16[1280,5120]{1,0:T(8,128)(2,1)} custom-call(s32[1,4]{1,0:T(1,128)S(1)} %copy-done.2, s32[1,4]{1,0:T(1,128)S(1)} %copy-done.3, f32[4]{0:T(128)S(1)} %copy-done.4, bf16[512,1280]{1,0:T(8,128)(2,1)S(1)} %bitcast.3, bf16[4,512,1280]{2,1,0:T(8,128)(2,1)S(1)} %bitcast.2), custom_call_target="tpu_custom_call" | custom-call | tf_op jit(solution)/shard_map/tiles/pallas_call | solution.py:311
Async XLA Ops:
  2.3 1.3 %copy-start = (bf16[64,10240]{1,0:T(8,128)(2,1)S(1)}, bf16[64,10240]{1,0:T(8,128)(2,1)}, u32[]{:S(2)}) copy-start(bf16[64,10240]{1,0:T(8,128)(2,1)} %maps_ref.3) | copy-start | bytes 3932164
  3.6 1.1 %copy-start.1 = (bf16[2,2,64,1280]{3,2,1,0:T(8,128)(2,1)S(1)}, bf16[2,2,64,1280]{3,2,1,0:T(8,128)(2,1)}, u32[]{:S(2)}) copy-start(bf16[2,2,64,1280]{3,2,1,0:T(8,128)(2,1)} %window.1.held_ref) | copy-start | bytes 1966084
  65.1 0.7 copy-start.2
  65.7 0.7 copy-start.3
  66.4 0.7 copy-start.4

commit v2 on v1

v2 whole, which is shorter than its diff:
```python
import functools

import jax
import jax.numpy as jnp
from jax import lax
from jax.experimental import pallas as pl
from jax.experimental.pallas import tpu as pltpu
from jax.sharding import PartitionSpec as P

MESH = pl.DeviceIdType.MESH
WINDOW = 4
CORES = 2
ALONG_Z = 4


def gather_kernel(
    row_count, col_count, window_ref, maps_ref, own_ref, panels_ref,
    maps, for_twin, mine, from_twin, summed, from_y, piece,
    twin_send, twin_recv, ysum_send, ysum_recv,
    z_send, x_send, y_send, core_send, panel_recv,
    own_send, own_recv, local_sem,
):
    ny, nx, nz = row_count // CORES, col_count // ALONG_Z, ALONG_Z
    row, col = lax.axis_index("row"), lax.axis_index("col")
    y, core = row // CORES, row % CORES
    z, x = col // nx, col % nx
    twin = y * CORES + (1 - core)
    width = own_ref.shape[2]
    part = panels_ref.shape[3]

    load_maps = pltpu.make_async_copy(maps_ref, maps, local_sem.at[2])
    load_maps.start()

    def row_of(d):
        return lax.rem(y + d, ny) * CORES + core

    barrier = pltpu.get_barrier_semaphore()
    peers = [(row, lax.rem(col + d, col_count)) for d in range(1, col_count)]
    peers += [(twin, col)] + [(row_of(d), col) for d in range(1, ny)]
    for peer in peers:
        pl.semaphore_signal(barrier, inc=1, device_id=peer, device_id_type=MESH)

    last = row_count * col_count - 1
    is_middle, rank, seen = [], [], 0
    for t in range(WINDOW):
        block = window_ref[t]
        is_middle.append(jnp.minimum(block, 1) * jnp.minimum(last - block, 1))
        rank.append(seen)
        seen = seen + is_middle[t]

    def masked(slot, offset):
        block = jnp.int32(0)
        for t in range(WINDOW):
            chosen = is_middle[t] * (1 - jnp.minimum(jnp.abs(rank[t] + 1 - slot), 1))
            block = block + chosen * window_ref[t]
        block = block + last * (1 - jnp.minimum(jnp.abs(slot - (WINDOW - 1)), 1))
        found = jnp.zeros((maps.shape[0], part), jnp.float32)
        for j in range(col_count):
            here = 1 - jnp.minimum(jnp.abs(block - (row * col_count + j)), 1)
            columns = maps[:, pl.ds(pl.multiple_of(j * width + offset, 128), part)]
            found = found + columns.astype(jnp.float32) * here.astype(jnp.float32)
        return found.astype(jnp.bfloat16)

    pl.semaphore_wait(barrier, len(peers))

    started = []

    def send(src, dst, send_sem, recv_sem, device):
        copy = pltpu.make_async_remote_copy(
            src_ref=src, dst_ref=dst, send_sem=send_sem, recv_sem=recv_sem,
            device_id=device, device_id_type=MESH,
        )
        copy.start()
        return copy

    def send_own(d):
        dest = lax.rem(col + d, col_count)
        columns = pl.ds(pl.multiple_of(dest * width, 128), width)
        started.append(send(
            maps_ref.at[:, columns], own_ref.at[col],
            own_send.at[d], own_recv.at[col], (row, dest),
        ))

    pending = list(range(1, col_count))
    pending.sort(key=lambda d: -abs(d - col_count // 2))
    pending = pending[::-1]

    def send_some(count):
        for _ in range(min(count, len(pending))):
            send_own(pending.pop(0))

    def slot(r, c):
        return panels_ref.at[r, c]

    def arrived(r, c):
        pltpu.make_async_remote_copy(
            src_ref=slot(r, c), dst_ref=slot(r, c), send_sem=core_send.at[r, c],
            recv_sem=panel_recv.at[r, c], device_id=(row, col), device_id_type=MESH,
        ).wait_recv()

    def out(src, r, c, send_sem, device, waiting):
        copy = pltpu.make_async_remote_copy(
            src_ref=src, dst_ref=slot(r, c), send_sem=send_sem,
            recv_sem=panel_recv.at[r, c], device_id=device, device_id_type=MESH,
        )
        if waiting:
            copy.wait_send()
        else:
            copy.start()

    def z_out(src, zz, up, waiting):
        to = z + 1 if up else z - 1

        @pl.when(to < nz if up else to >= 0)
        def _():
            c = zz * nx + x
            out(src, row, c, z_send.at[int(up), zz], (row, to * nx + x), waiting)

    def x_out(src, zz, waiting):
        c = zz * nx + x
        for d in range(1, nx):
            out(src, row, c, x_send.at[d, zz], (row, z * nx + lax.rem(x + d, nx)), waiting)

    def y_out(src, c, waiting):
        for d in range(1, ny):
            out(src, row, c, y_send.at[d, c], (row_of(d), col), waiting)

    def core_out(src, r, c, waiting):
        out(src, r, c, core_send.at[r, c], (twin, col), waiting)

    def at_z(d, body):
        if d == 0:
            body(z, None)
            return

        @pl.when(z >= d)
        def _():
            body(z - d, True)

        @pl.when(z + d < nz)
        def _():
            body(z + d, False)

    def own_event(src, waiting):
        z_out(src, z, True, waiting)
        z_out(src, z, False, waiting)
        y_out(src, col, waiting)
        x_out(src, z, waiting)
        core_out(src, row, col, waiting)

    def z_event(waiting, zz, up):
        c = zz * nx + x
        src = slot(row, c)
        if not waiting:
            arrived(row, c)
        z_out(src, zz, up, waiting)
        y_out(src, c, waiting)
        x_out(src, zz, waiting)
        core_out(src, row, c, waiting)

    def x_event(waiting, zz, up):
        for d in range(1, nx):
            c = zz * nx + lax.rem(x + d, nx)
            if not waiting:
                arrived(row, c)
            y_out(slot(row, c), c, waiting)
            core_out(slot(row, c), row, c, waiting)

    def y_event(waiting, own_x, zz, up):
        for dx in ([0] if own_x else range(1, nx)):
            c = zz * nx + lax.rem(x + dx, nx)
            for d in range(1, ny):
                r = row_of(d)
                if not waiting:
                    arrived(r, c)
                core_out(slot(r, c), r, c, waiting)

    def events(waiting):
        if waiting:
            own_event(piece, True)
        for d in range(1, nz):
            at_z(d, functools.partial(z_event, waiting))
            at_z(d - 1, functools.partial(x_event, waiting))
            if not waiting:
                send_some(2 if d < nz - 2 else col_count)
        at_z(nz - 1, functools.partial(x_event, waiting))
        for d in range(nz):
            at_z(d, functools.partial(y_event, waiting, True))
            at_z(d, functools.partial(y_event, waiting, False))

    keep_own = pltpu.make_async_copy(
        maps_ref.at[:, pl.ds(pl.multiple_of(col * width, 128), width)], own_ref.at[col], local_sem.at[0]
    )
    keep_own.start()
    direct = part == width and row_count == WINDOW
    ends = lax.rem(row, row_count - 1) == 0

    def y_sum(d):
        return pltpu.make_async_remote_copy(
            src_ref=summed.at[d], dst_ref=from_y.at[ny - d], send_sem=ysum_send.at[d],
            recv_sem=ysum_recv.at[ny - d], device_id=(row_of(d), col), device_id_type=MESH,
        )

    if direct:
        first = pl.multiple_of((row // (row_count - 1)) * ((col_count - 1) * width), 128)
        held_piece = maps_ref.at[:, pl.ds(first, width)]

        @pl.when(ends)
        def _():
            own_event(held_piece, False)
            pltpu.make_async_copy(held_piece, slot(row, col), local_sem.at[1]).start()

        send_some(2)
        load_maps.wait()
        for_twin[0] = masked(1 + core, 0)
        mine[0] = masked(2 - core, 0)
        twin_copy = send(for_twin, from_twin, twin_send, twin_recv, (twin, col))
        twin_copy.wait_recv()
        summed[1] = mine[0] + from_twin[0]

        @pl.when(ends)
        def _():
            y_sum(1).start()

        @pl.when(jnp.logical_not(ends))
        def _():
            y_sum(1).wait_recv()
            piece[...] = summed[1] + from_y[1]
            own_event(piece, False)
            pltpu.make_async_copy(piece, slot(row, col), local_sem.at[1]).start()
    else:
        load_maps.wait()
        for d in range(ny):
            for k, held in ((1 - core, for_twin), (core, mine)):
                first = (lax.rem(y + d, ny) * CORES + k) * part
                held[d] = masked(first // width, lax.rem(first, width))
        twin_copy = send(for_twin, from_twin, twin_send, twin_recv, (twin, col))
        twin_copy.wait_recv()
        for d in range(ny):
            summed[d] = mine[d] + from_twin[d]
        for d in range(1, ny):
            y_sum(d).start()
        send_some(2)
        total = summed[0]
        for d in range(1, ny):
            y_sum(d).wait_recv()
            total = total + from_y[ny - d]
        piece[...] = total
        own_event(piece, False)
        pltpu.make_async_copy(piece, slot(row, col), local_sem.at[1]).start()
    send_some(2)
    events(False)

    for d in range(ny):
        r = lax.rem(y + d, ny) * CORES + (1 - core)

        @pl.loop(0, col_count)
        def _(c):
            arrived(r, c)

    for d in range(1, col_count):
        source = lax.rem(col + d, col_count)
        pltpu.make_async_remote_copy(
            src_ref=own_ref.at[source], dst_ref=own_ref.at[source], send_sem=own_send.at[d],
            recv_sem=own_recv.at[source], device_id=(row, source), device_id_type=MESH,
        ).wait_recv()
    twin_copy.wait_send()
    for copy in started:
        copy.wait_send()
    if direct:
        @pl.when(ends)
        def _():
            y_sum(1).wait_send()
    else:
        for d in range(1, ny):
            y_sum(d).wait_send()
    events(True)
    keep_own.wait()
    pltpu.make_async_copy(piece, slot(row, col), local_sem.at[1]).wait()


def gather(mock_maps, window_blocks, row_count, col_count):
    mocks = mock_maps.shape[0]
    width = mock_maps.shape[1] // col_count
    part = WINDOW * width // row_count
    ny = row_count // CORES
    nx = col_count // ALONG_Z
    dma = pltpu.SemaphoreType.DMA
    shares = 1 if part == width else ny
    return pl.pallas_call(
        functools.partial(gather_kernel, row_count, col_count),
        out_shape=(
            jax.ShapeDtypeStruct((col_count, mocks, width), jnp.bfloat16),
            jax.ShapeDtypeStruct((row_count, col_count, mocks, part), jnp.bfloat16),
        ),
        in_specs=[pl.BlockSpec(memory_space=pltpu.SMEM), pl.BlockSpec(memory_space=pl.ANY)],
        out_specs=(pl.BlockSpec(memory_space=pl.ANY), pl.BlockSpec(memory_space=pl.ANY)),
        scratch_shapes=[
            pltpu.VMEM(mock_maps.shape, jnp.bfloat16),
            pltpu.VMEM((shares, mocks, part), jnp.bfloat16),
            pltpu.VMEM((shares, mocks, part), jnp.bfloat16),
            pltpu.VMEM((shares, mocks, part), jnp.bfloat16),
            pltpu.VMEM((ny, mocks, part), jnp.bfloat16),
            pltpu.VMEM((ny, mocks, part), jnp.bfloat16),
            pltpu.VMEM((mocks, part), jnp.bfloat16),
            dma, dma, dma((ny,)), dma((ny,)),
            dma((2, ALONG_Z)), dma((nx, ALONG_Z)), dma((ny, col_count)),
            dma((row_count, col_count)), dma((row_count, col_count)),
            dma((col_count,)), dma((col_count,)), dma((3,)),
        ],
        compiler_params=pltpu.CompilerParams(
            collective_id=0, has_side_effects=True, vmem_limit_bytes=60 * 2**20
        ),
        name="gather",
    )(window_blocks, mock_maps)


def ordered_slot(window_ref, last, slot):
    block = window_ref[slot]
    rank = jnp.int32(1)
    for t in range(WINDOW):
        middle = (t < slot) & (window_ref[t] != 0) & (window_ref[t] != last)
        rank = rank + middle.astype(jnp.int32)
    return jnp.where(block == 0, 0, jnp.where(block == last, WINDOW - 1, rank))


ONES = 16
HALVES = 2


def tile_kernel(parts, window_ref, kept_ref, index_ref, table_ref, own_ref, panel_ref, out_ref, own_t):
    step, half = pl.program_id(0), pl.program_id(1)
    slot = step // parts
    count, width = own_ref.shape
    rows = width // HALVES

    @pl.when((step == 0) & (half == 0))
    def _():
        for h in range(HALVES):
            own_t[h, :ONES] = jnp.ones((ONES, count), jnp.bfloat16)
            own_t[h, ONES:] = own_ref[:, h * rows:(h + 1) * rows].T

    kept = kept_ref[0, slot] > 0

    @pl.when(kept)
    def _():
        scale = table_ref[index_ref[0, slot]] / (count - 1)
        own_sum = jnp.dot(
            own_t[half, ONES:], jnp.ones((count, 128), jnp.bfloat16), preferred_element_type=jnp.float32
        )
        for first in range(0, out_ref.shape[1], 256):
            panel = panel_ref[0, :, first:first + 256]
            products = jnp.dot(own_t[half], panel, preferred_element_type=jnp.float32)
            panel_mean = products[:1] / count
            for part in range(0, panel.shape[1], 128):
                here = slice(part, part + 128)
                centred = products[ONES:, here] - own_sum * panel_mean[:, here]
                out_ref[:, first + part:first + part + 128] = (scale * centred).astype(jnp.bfloat16)

    @pl.when(jnp.logical_not(kept))
    def _():
        out_ref[...] = jnp.zeros_like(out_ref)


def tiles(own, panels, window_blocks, kept_tiles, taper_index, taper_table, last):
    count, width = own.shape
    steps, _, part = panels.shape
    parts = width // part
    smem = pl.BlockSpec(memory_space=pltpu.SMEM)

    def panel_index(i, h, window_ref):
        return ordered_slot(window_ref, last, i // parts) * parts + i % parts, 0, 0

    return pl.pallas_call(
        functools.partial(tile_kernel, parts),
        out_shape=jax.ShapeDtypeStruct((width, steps * part), jnp.bfloat16),
        grid_spec=pltpu.PrefetchScalarGridSpec(
            num_scalar_prefetch=1,
            grid=(steps, HALVES),
            in_specs=[
                smem, smem, smem,
                pl.BlockSpec((count, width), lambda i, h, w: (0, 0)),
                pl.BlockSpec((1, count, part), panel_index),
            ],
            out_specs=pl.BlockSpec((width // HALVES, part), lambda i, h, w: (h, i)),
            scratch_shapes=[pltpu.VMEM((HALVES, ONES + width // HALVES, count), jnp.bfloat16)],
        ),
        compiler_params=pltpu.CompilerParams(
            dimension_semantics=("arbitrary", "arbitrary"), vmem_limit_bytes=60 * 2**20
        ),
        name="tiles",
    )(window_blocks, kept_tiles, taper_index, taper_table, own, panels)


def per_device(row_count, col_count, mock_maps, window_blocks, kept_tiles, taper_index, taper_table):
    own, panels = gather(mock_maps, window_blocks, row_count, col_count)
    own = own.reshape(-1, own.shape[-1])
    panels = panels.reshape(panels.shape[0], -1, panels.shape[-1])
    last = row_count * col_count - 1
    return tiles(own, panels, window_blocks, kept_tiles, taper_index, taper_table, last)


def solution(mesh):
    in_specs = (P("col", "row"), P(), P(("row", "col"), None), P(("row", "col"), None), P())
    out_specs = P(("row", "col"), None)
    return jax.shard_map(
        functools.partial(per_device, mesh.shape["row"], mesh.shape["col"]),
        mesh=mesh, in_specs=in_specs, out_specs=out_specs, check_vma=False,
    )
```

time: 78 us -> 75.2 us (0.964)
  the two profiles are of different devices: /device:TPU:0 before, /device:TPU:1 now
where the time goes in v2:
time: 75.2 us; the launch traced here: 74.1 us
  Pallas kernels  74 us (98%)
    pallas_call x1, Pallas kernels, gather(): pl.pallas_call(functools.partial(gather_kernel, row_count, col_count), ou...  59.3 us
    pallas_call x1, Pallas kernels, tiles(): pl.pallas_call(functools.partial(tile_kernel, parts), out_shape=jax.Shape...  14.8 us

profile of v2, /device:TPU:1, one launch (start us, length us, event | category | flops | bytes accessed | tf_op | source)
XLA Modules:
  0.0 74.1 jit_solution(17124041457306920606)
XLA Ops:
  0.0 59.3 %gather.1 = (bf16[8,64,1280]{2,1,0:T(8,128)(2,1)}, bf16[4,8,64,1280]{3,2,1,0:T(8,128)(2,1)}) custom-call(s32[4]{0:T(128)} %window_ref.3, bf16[64,10240]{1,0:T(8,128)(2,1)} %maps_ref.1), custom_call_target="tpu_custom_call" | custom-call | tf_op jit(solution)/shard_map/gather/pallas_call | solution.py:290
  59.3 14.8 %tiles.1 = bf16[1280,5120]{1,0:T(8,128)(2,1)} custom-call(s32[4]{0:T(128)} %window_ref.3, s32[1,4]{1,0:T(1,128)} %kept_ref.1, s32[1,4]{1,0:T(1,128)} %index_ref.1, f32[4]{0:T(128)} %table_ref.1, bf16[512,1280]{1,0:T(8,128)(2,1)} %bitcast.3, bf16[4,512,1280]{2,1,0:T(8,128)(2,1)} %bitcast.2), custom_call_target="tpu_custom_call" | custom-call | tf_op jit(solution)/shard_map/tiles/pallas_call | solution.py:374
